TPU v7x, 32 devices: a whole 2x2x4 slice. The times are simulated.
32 devices in a mesh: groups: 2 (over y), enrol: 4 (over z), probe: 4 (over x, core).
Axes of the slice: x: 2, y: 2, z: 4, core: 2. Of those that a mesh axis runs over, the one named last changes fastest.
Arguments:
- images: float32 [16384, 512], P(('groups', 'enrol', 'probe')), parts along dimension 0, may hold values from -6 to 6
- w_first: float32 [512, 2048], replicated, may hold values from -0.25 to 0.25
- w_second: float32 [2048, 256], replicated, may hold values from -0.125 to 0.125
- calib_scale: float32 [1], replicated, may hold values from 5 to 20
- calib_bias: float32 [1], replicated, may hold values from -2 to 2
- template_slot: int32 [16384], P(('groups', 'enrol', 'probe')), parts along dimension 0, may hold values from 0 to 191
- media_counts: int32 [32, 16], P(('groups', 'enrol', 'probe')), parts along dimension 0, may hold values from 1 to 64, as said below
Outputs:
- scores: bfloat16 [4096, 1024], P(('groups', 'enrol'), 'probe'), parts along dimension 0
There are 2 independent parts, one for each index of `groups`. A program takes and returns all parts, laid end to end along the dimension named above; an argument that names none is the same for every part. Nothing has to cross between parts.
Inputs may be any that keep to these rules, and one draw needn't show every extreme that they name: `media_counts`: each row sums to 512; in every draw one owner receives exactly 64 images from every device.
All inputs are finite; a program needn't handle non-finite values.
Results may differ from a plain program's by a relative error of at most 0.001.
Values sent between devices are 32-bit elements; how exact they have to be, the bound alone decides.
A program may use at most 64 MiB of HBM per device.

v0:
```python
import jax
import jax.numpy as jnp
from jax import lax
from jax.sharding import PartitionSpec as P

ET_OWN = 128
PT_OWN = 64


HIGH = lax.Precision.HIGHEST


def unit_rows(table):
    return table * lax.rsqrt(jnp.sum(table * table, axis=-1, keepdims=True) + 1e-06)


def shards(images, w_first, w_second, calib_scale, calib_bias, template_slot, media_counts):
    owners = media_counts.shape[1]
    local_images = images.shape[0]
    capacity = 2 * local_images // owners
    width = w_second.shape[1]
    hidden = jax.nn.gelu(
        jnp.dot(images, w_first, precision=HIGH, preferred_element_type=jnp.float32)
    )
    feature = jnp.dot(hidden, w_second, precision=HIGH, preferred_element_type=jnp.float32)
    embedding = unit_rows(feature)
    counts = media_counts[0]
    starts = jnp.cumsum(counts) - counts
    offsets = jnp.arange(capacity, dtype=jnp.int32)
    filled = offsets[None, :] < counts[:, None]
    picked = jnp.where(filled, starts[:, None] + offsets[None, :], 0).reshape(-1)
    send_rows = embedding[picked].reshape(owners, capacity, width) * filled[:, :, None].astype(
        jnp.float32
    )
    send_slots = jnp.where(filled, template_slot[picked].reshape(owners, capacity), -1)
    got_rows, got_slots = (
        lax.all_to_all(send_rows, ("enrol", "probe"), split_axis=0, concat_axis=0, tiled=True),
        lax.all_to_all(send_slots, ("enrol", "probe"), split_axis=0, concat_axis=0, tiled=True),
    )
    got_rows = got_rows.reshape(owners * capacity, width)
    got_slots = got_slots.reshape(owners * capacity)
    slot_count = ET_OWN + PT_OWN
    selector = (got_slots[None, :] == jnp.arange(slot_count, dtype=jnp.int32)[:, None]).astype(
        jnp.float32
    )
    pooled = jnp.dot(selector, got_rows, precision=HIGH, preferred_element_type=jnp.float32)
    templates = unit_rows(pooled)
    enrol_own = templates[:ET_OWN]
    probe_own = templates[ET_OWN:]
    enrol_block = lax.all_gather(enrol_own, "probe", axis=0, tiled=True)
    slope = calib_scale[0]
    offset = calib_bias[0]
    cosine = jnp.dot(
        enrol_block,
        lax.all_gather(probe_own, "enrol", axis=0, tiled=True).T,
        precision=HIGH,
        preferred_element_type=jnp.float32,
    )
    return jax.nn.sigmoid(slope * cosine + offset).astype(jnp.bfloat16)


def solution(mesh):
    return jax.shard_map(
        shards,
        mesh=mesh,
        in_specs=(
            P(("groups", "enrol", "probe"), None),
            P(),
            P(),
            P(),
            P(),
            P(("groups", "enrol", "probe")),
            P(("groups", "enrol", "probe"), None),
        ),
        out_specs=P(("groups", "enrol"), "probe"),
        check_vma=False,
    )
```

profile of v0, /device:TPU:0, one launch (start us, length us, event | category | flops | bytes accessed | tf_op | source)
XLA Modules:
  0.0 92.6 jit_solution(2711061738317746428)
XLA Ops:
  0.0 0.0 copy-start
  0.0 0.0 copy-start.2
  0.0 0.0 copy-start.1
  0.0 0.9 copy.10
  0.9 0.1 reduce
  1.0 0.7 bitcast_subtract_fusion
  1.7 0.7 add_select_fusion
  2.4 0.1 select_n.37
  2.5 6.2 %gather_fusion = s32[1024]{0:T(1024)S(1)} fusion(s32[512]{0:T(512)} %param.12, s32[1024]{0:T(1024)S(1)} %broadcast_clamp_fusion), kind=kCustom, calls=%fused_computation | custom fusion | bytes 12288 | tf_op jit(solution)/shard_map/gather | solution.py:35
  8.7 0.1 reshape.184
  8.8 0.0 copy-done.2
  8.8 0.7 compare_select_fusion
  9.5 7.4 %all-to-all-start = ((s32[16,1,64]{2,1,0:T(1,128)}), s32[16,1,64]{2,1,0:T(1,128)S(1)}, u32[]{:S(2)}, u32[]{:S(2)}) async-start(s32[16,1,64]{2,1,0:T(1,128)} %compare_select_fusion), calls=%async_computation | async-start | bytes 16384 | tf_op jit(solution)/shard_map/all_to_all | solution.py:38
  16.9 0.1 fusion.21
  16.9 0.0 copy-done.1
  16.9 8.8 %fusion.26 = f32[512,2048]{1,0:T(8,128)S(1)} fusion(f32[512,512]{1,0:T(8,128)S(1)} %copy-done.1, f32[512,2048]{1,0:T(8,128)} %param.8), kind=kOutput, calls=%fused_computation.43 | convolution fusion | flops 6442450944 | bytes 9437184 | tf_op jit(solution)/shard_map/dot_general | solution.py:23
  25.7 0.0 copy-done
  25.7 5.1 %multiply_reduce_fusion = (f32[512]{0:T(512)S(1)}, f32[512,256]{0,1:T(8,128)S(1)}) fusion(f32[2048,256]{1,0:T(8,128)S(1)} %copy-done, f32[512,2048]{1,0:T(8,128)S(1)} %fusion.26), kind=kOutput, calls=%fused_computation.25 | convolution fusion | flops 3229875712 | bytes 6817792 | tf_op jit(solution)/shard_map/dot_general | solution.py:25
  30.9 0.1 broadcast_multiply_fusion.1
  30.9 0.2 copy.11
  31.1 4.7 %gather_fusion.1 = f32[1024,256]{1,0:T(8,128)} fusion(f32[512,256]{1,0:T(8,128)S(1)} %copy.11, s32[1024]{0:T(1024)S(1)} %broadcast_clamp_fusion), kind=kCustom, calls=%fused_computation.1 | custom fusion | bytes 2101248 | tf_op jit(solution)/shard_map/gather | solution.py:32
  35.8 2.4 %broadcast_multiply_fusion = f32[16,64,256]{2,1,0:T(8,128)} fusion(f32[16,64,256]{2,1,0:T(8,128)} %bitcast.16, f32[16,64]{1,0:T(8,128)S(1)} %fusion.21), kind=kLoop, calls=%fused_computation.24 | loop fusion | flops 262144 | bytes 2101248 | tf_op jit(solution)/shard_map/mul | solution.py:32
  38.2 0.0 all-to-all-done
  38.2 6.0 %all-to-all-start.1 = ((f32[16,64,256]{2,1,0:T(8,128)}), f32[16,64,256]{2,1,0:T(8,128)S(1)}, u32[]{:S(2)}, u32[]{:S(2)}) async-start(f32[16,64,256]{2,1,0:T(8,128)} %broadcast_multiply_fusion), calls=%async_computation.1 | async-start | bytes 2097152 | tf_op jit(solution)/shard_map/all_to_all | solution.py:37
  45.5 0.5 broadcast.96
  46.0 0.7 reduce.4
  46.7 0.1 eq.15
  46.8 20.4 %all-to-all-done.1 = f32[16,64,256]{2,1,0:T(8,128)S(1)} async-done(((f32[16,64,256]{2,1,0:T(8,128)}), f32[16,64,256]{2,1,0:T(8,128)S(1)}, u32[]{:S(2)}, u32[]{:S(2)}) %all-to-all-start.1) | async-done | bytes 1048608 | tf_op jit(solution)/shard_map/all_to_all | solution.py:37
  67.2 0.8 multiply_reduce_fusion.1
  67.9 0.1 broadcast_multiply_fusion.2
  68.1 7.8 %all_gather.6 = f32[512,256]{1,0:T(8,128)S(1)} all-gather(f32[128,256]{1,0:T(8,128)S(1)} %slice.12), channel_id=1, replica_groups=mesh['groups'=2,'enrol'=4,'probe'=4] {'probe'}, dimensions={0}, use_global_device_ids=true | all-gather | bytes 655360 | tf_op jit(solution)/shard_map/all_gather | solution.py:50
  75.9 15.4 %all_gather.7 = f32[256,256]{1,0:T(8,128)S(1)} all-gather(f32[64,256]{1,0:T(8,128)S(1)} %slice.13), channel_id=1, replica_groups=mesh['groups'=2,'enrol'=4,'probe'=4] {'enrol'}, dimensions={0}, use_global_device_ids=true | all-gather | bytes 327680 | tf_op jit(solution)/shard_map/all_gather | solution.py:55
  91.2 1.4 %fusion.18 = bf16[512,256]{1,0:T(8,128)(2,1)} fusion(f32[512,256]{1,0:T(8,128)S(1)} %all_gather.6, f32[256,256]{1,0:T(8,128)S(1)} %all_gather.7, f32[]{:T(128)} %bitcast.15, f32[]{:T(128)} %bitcast.14), kind=kOutput, calls=%fused_computation.21 | convolution fusion | flops 403439616 | bytes 1048584 | tf_op jit(solution)/shard_map/dot_general | solution.py:53
  (7 shorter events, 0.1 us)
Async XLA Ops:
  0.0 25.7 %copy-start = (f32[2048,256]{1,0:T(8,128)S(1)}, f32[2048,256]{1,0:T(8,128)}, u32[]{:S(2)}) copy-start(f32[2048,256]{1,0:T(8,128)} %param.9) | copy-start | bytes 6291460
  0.0 8.8 %copy-start.2 = (s32[1,16]{1,0:T(1,128)S(1)}, s32[1,16]{1,0:T(1,128)}, u32[]{:S(2)}) copy-start(s32[1,16]{1,0:T(1,128)} %param.13) | copy-start | bytes 196
  0.0 16.9 %copy-start.1 = (f32[512,512]{1,0:T(8,128)S(1)}, f32[512,512]{1,0:T(8,128)}, u32[]{:S(2)}) copy-start(f32[512,512]{1,0:T(8,128)} %param.7) | copy-start | bytes 3145732
  9.5 28.7 %all-to-all-start = ((s32[16,1,64]{2,1,0:T(1,128)}), s32[16,1,64]{2,1,0:T(1,128)S(1)}, u32[]{:S(2)}, u32[]{:S(2)}) async-start(s32[16,1,64]{2,1,0:T(1,128)} %compare_select_fusion), calls=%async_computation | async-start | bytes 16384 | tf_op jit(solution)/shard_map/all_to_all | solution.py:38
  38.2 29.0 %all-to-all-start.1 = ((f32[16,64,256]{2,1,0:T(8,128)}), f32[16,64,256]{2,1,0:T(8,128)S(1)}, u32[]{:S(2)}, u32[]{:S(2)}) async-start(f32[16,64,256]{2,1,0:T(8,128)} %broadcast_multiply_fusion), calls=%async_computation.1 | async-start | bytes 2097152 | tf_op jit(solution)/shard_map/all_to_all | solution.py:37
where the time goes:
time: 93 us; the launch traced here: 92.6 us
  blocking collectives  23.2 us (25%)
  waiting for transfers between devices  20.4 us (22%)
  matrix products  16 us (17%)
  starting transfers between devices  13.4 us (14%)
  local copies, waits for them, and re-layouts  12.7 us (14%)
  other arithmetic  5.57 us (6%)
  between operations  1.41 us (2%)
    all_to_all x1, waiting for transfers between devices, shards(): lax.all_to_all(send_rows, ('enrol', 'probe'), split_axis=0, concat_axis=0...  20.4 us
    all_gather x1, blocking collectives, shards(): lax.all_gather(probe_own, 'enrol', axis=0, tiled=True)  15.4 us
    dot_general x1, matrix products, shards(): jnp.dot(images, w_first, precision=HIGH, preferred_element_type=jnp.float32)  8.8 us
    all_gather x1, blocking collectives, shards(): enrol_block = lax.all_gather(enrol_own, 'probe', axis=0, tiled=True)  7.78 us
    all_to_all x1, starting transfers between devices, shards(): lax.all_to_all(send_slots, ('enrol', 'probe'), split_axis=0, concat_axis=...  7.36 us
    gather x1, local copies, waits for them, and re-layouts, shards(): template_slot[picked].reshape(owners, capacity)  6.18 us
    all_to_all x1, starting transfers between devices, shards(): lax.all_to_all(send_rows, ('enrol', 'probe'), split_axis=0, concat_axis=0...  6 us
    dot_general x1, matrix products, shards(): jnp.dot(hidden, w_second, precision=HIGH, preferred_element_type=jnp.floa...  5.09 us
  transfers between devices with their start and end apart: 2, of which 1 were waited for; matrix products, arithmetic and copies ran while one was open for 24% of the time, Pallas kernels for 0%

commit v1 on v0

v1 whole, which is shorter than its diff:
```python
import functools

import jax
import jax.numpy as jnp
from jax import lax
from jax.experimental import pallas as pl
from jax.experimental.pallas import tpu as pltpu
from jax.sharding import PartitionSpec as P

ET_OWN = 128
PT_OWN = 64
LANES = 128
MESH = pl.DeviceIdType.MESH
F32 = jnp.float32
BF16 = jnp.bfloat16


def split(x):
    high = x.astype(BF16)
    return high, (x - high.astype(F32)).astype(BF16)


def one_hot(mask):
    return jnp.where(mask, 1.0, 0.0).astype(BF16)


def nt(a, b):
    return lax.dot_general(a, b, (((1,), (1,)), ((), ())), preferred_element_type=F32)


def kernel(
    ne, np_, chunk,
    images, w_first, w_second, scale, bias, slots, counts,
    out,
    w1, w2, gather, catted, slot_tiles, slot_send, slot_recv, send, recv, pool, enrol, probe,
    w1_sem, w2_sem, ss_sem, sr_sem, rs_sem, rr_sem, es_sem, er_sem, ps_sem, pr_sem,
):
    n = ne * np_
    images_here = images.shape[0]
    cap = 2 * images_here // n
    total = n * cap
    width = w_second.shape[1]
    g, e, p = lax.axis_index("groups"), lax.axis_index("enrol"), lax.axis_index("probe")
    me = e * np_ + p

    def device(o):
        return (g, o // np_, lax.rem(o, np_))

    barrier = pltpu.get_barrier_semaphore()

    def greet(k, c):
        pl.semaphore_signal(
            barrier, inc=1, device_id=device(lax.rem(me + k, n)), device_id_type=MESH
        )
        return c

    lax.fori_loop(1, n, greet, 0)

    chunks = w1.shape[0]
    loads = []
    for c in range(chunks):
        a = pltpu.make_async_copy(w_first.at[:, pl.ds(c * chunk, chunk)], w1.at[c], w1_sem.at[c])
        b = pltpu.make_async_copy(w_second.at[pl.ds(c * chunk, chunk), :], w2.at[c], w2_sem.at[c])
        a.start()
        b.start()
        loads.append((a, b))

    at = lax.broadcasted_iota(jnp.int32, (1, images_here), 1)

    def place(k, carry):
        dest, end = carry
        end = end + counts[0, k]
        return dest + jnp.where(at >= end, cap - counts[0, k], 0), end

    dest, _ = lax.fori_loop(0, n, place, (at, jnp.int32(0)), unroll=n <= 16)
    rows = lax.broadcasted_iota(jnp.int32, (LANES, images_here), 0)
    wanted = jnp.broadcast_to((slots[...] + 1).astype(F32), (8, images_here)).astype(BF16)
    for j in range(total // LANES):
        tile = one_hot(rows + j * LANES == dest)
        gather[pl.ds(j * LANES, LANES), :] = tile
        slot_tiles[j] = nt(wanted, tile)

    pl.semaphore_wait(barrier, n - 1)

    my_off = lax.rem(me * cap, LANES)
    lane = lax.broadcasted_iota(jnp.int32, (8, LANES), 1)
    mine = (lane >= my_off) & (lane < my_off + cap)

    def slot_row(o):
        tile = slot_tiles[(o * cap) // LANES]
        shift = lax.rem(my_off - lax.rem(o * cap, LANES) + LANES, LANES)
        return jnp.where(mine, pltpu.roll(tile, shift, 1), 0.0)

    def slot_copy(o, source):
        return pltpu.make_async_remote_copy(
            src_ref=slot_send.at[o], dst_ref=slot_recv.at[source],
            send_sem=ss_sem.at[o], recv_sem=sr_sem.at[source],
            device_id=device(o), device_id_type=MESH,
        )

    def row_copy(o, source):
        return pltpu.make_async_remote_copy(
            src_ref=send.at[o], dst_ref=recv.at[source],
            send_sem=rs_sem.at[o], recv_sem=rr_sem.at[source],
            device_id=device(o), device_id_type=MESH,
        )

    def send_slots(k, c):
        o = lax.rem(me + k, n)
        slot_send[o] = slot_row(o)
        slot_copy(o, me).start()
        return c

    lax.fori_loop(1, n, send_slots, 0)
    slot_recv[me] = slot_row(me)

    xh, xl = split(images[...])
    x3 = jnp.concatenate([xh, xl, xh], axis=1)
    feature = None
    for c in range(chunks):
        loads[c][0].wait()
        ah, al = split(w1[c])
        hidden = jax.nn.gelu(
            jnp.dot(x3, jnp.concatenate([ah, ah, al], axis=0), preferred_element_type=F32)
        )
        hh, hl = split(hidden)
        loads[c][1].wait()
        bh, bl = split(w2[c])
        part = jnp.dot(
            jnp.concatenate([hh, hl, hh], axis=1),
            jnp.concatenate([bh, bh, bl], axis=0),
            preferred_element_type=F32,
        )
        feature = part if feature is None else feature + part
    embedding = feature * lax.rsqrt(jnp.sum(feature * feature, axis=-1, keepdims=True) + 1e-06)
    h, l = split(embedding)
    catted[:, :width] = h
    catted[:, width:] = l

    half = ne // 2
    here = e // half
    per_row = np_ * cap
    for t in range(ne):
        if t < half:
            er = (1 - here) * half + lax.rem(e + t, half)
        else:
            er = here * half + lax.rem(e + 1 + t - half, half)
        picked = jnp.dot(
            gather[pl.ds(pl.multiple_of(er * per_row, per_row), per_row), :],
            catted[...],
            preferred_element_type=F32,
        )
        picked = (picked[:, :width] + picked[:, width:]).reshape(np_, cap, width)
        send[pl.ds(er * np_, np_)] = picked
        if t < ne - 1:
            for k in range(np_):
                row_copy(er * np_ + lax.rem(p + k, np_), me).start()
        else:
            for k in range(1, np_):
                row_copy(er * np_ + lax.rem(p + k, np_), me).start()
            recv[me] = send[me]

    def slots_in(k, c):
        o = lax.rem(me + k, n)
        slot_copy(o, o).wait_recv()
        return c

    lax.fori_loop(1, n, slots_in, 0)
    owned = pool.shape[0]
    ids = lax.broadcasted_iota(jnp.int32, (owned, LANES), 0) + 1
    together = LANES // cap
    for j in range(total // LANES):
        tile = slot_recv[j * together]
        for k in range(1, together):
            tile = tile + slot_recv[j * together + k]
        pool[:, j * LANES:(j + 1) * LANES] = one_hot(tile[0:1].astype(jnp.int32) == ids)

    def rows_in(k, c):
        o = lax.rem(me + k, n)
        row_copy(o, o).wait_recv()
        return c

    lax.fori_loop(1, n, rows_in, 0)
    h, l = split(recv[...].reshape(total, width))
    pooled = jnp.dot(pool[...], jnp.concatenate([h, l], axis=1), preferred_element_type=F32)
    pooled = pooled[:, :width] + pooled[:, width:]
    templates = pooled * lax.rsqrt(jnp.sum(pooled * pooled, axis=-1, keepdims=True) + 1e-06)
    enrol[p] = templates[:ET_OWN]
    probe[e] = templates[ET_OWN:]

    def enrol_copy(k):
        to = lax.rem(p + k, np_)
        return to, pltpu.make_async_remote_copy(
            src_ref=enrol.at[p], dst_ref=enrol.at[p],
            send_sem=es_sem.at[to], recv_sem=er_sem.at[p],
            device_id=(g, e, to), device_id_type=MESH,
        )

    def enrol_arrival(o):
        return pltpu.make_async_remote_copy(
            src_ref=enrol.at[o], dst_ref=enrol.at[o],
            send_sem=es_sem.at[o], recv_sem=er_sem.at[o],
            device_id=(g, e, o), device_id_type=MESH,
        )

    def probe_copy(to, source):
        return pltpu.make_async_remote_copy(
            src_ref=probe.at[source], dst_ref=probe.at[source],
            send_sem=ps_sem.at[to], recv_sem=pr_sem.at[source],
            device_id=(g, to, p), device_id_type=MESH,
        )

    for k in range(ne - 1, 0, -1):
        probe_copy(lax.rem(e + k, ne), e).start()
    for k in range(np_ - 1, 0, -1):
        enrol_copy(k)[1].start()
    for k in range(1, ne):
        o = lax.rem(e + k, ne)
        probe_copy(o, o).wait_recv()
    for k in range(1, np_):
        enrol_arrival(lax.rem(p + k, np_)).wait_recv()

    ph, pl_ = split(probe[...].reshape(ne * PT_OWN, width))
    right = jnp.concatenate([ph, ph, pl_], axis=1)
    slope, offset = scale[0], bias[0]
    for k in range(np_):
        eh, el = split(enrol[k])
        cosine = nt(jnp.concatenate([eh, el, eh], axis=1), right)
        out[k * ET_OWN:(k + 1) * ET_OWN, :] = jax.nn.sigmoid(slope * cosine + offset).astype(BF16)

    def drain(k, c):
        o = lax.rem(me + k, n)
        slot_copy(o, me).wait_send()
        row_copy(o, me).wait_send()
        return c

    lax.fori_loop(1, n, drain, 0)
    for k in range(1, ne):
        probe_copy(lax.rem(e + k, ne), e).wait_send()
    for k in range(1, np_):
        enrol_copy(k)[1].wait_send()


def shards(ne, np_, images, w_first, w_second, calib_scale, calib_bias, template_slot, media_counts):
    n = ne * np_
    here, features = images.shape
    hidden, width = w_second.shape
    cap = 2 * here // n
    total = n * cap
    chunk = 256
    chunks = hidden // chunk
    vmem = pl.BlockSpec(memory_space=pltpu.VMEM)
    smem = pl.BlockSpec(memory_space=pltpu.SMEM)
    anywhere = pl.BlockSpec(memory_space=pl.ANY)
    dma = pltpu.SemaphoreType.DMA
    return pl.pallas_call(
        functools.partial(kernel, ne, np_, chunk),
        out_shape=jax.ShapeDtypeStruct((np_ * ET_OWN, ne * PT_OWN), BF16),
        in_specs=[vmem, anywhere, anywhere, smem, smem, vmem, smem],
        out_specs=vmem,
        scratch_shapes=[
            pltpu.VMEM((chunks, features, chunk), F32),
            pltpu.VMEM((chunks, chunk, width), F32),
            pltpu.VMEM((total, here), BF16),
            pltpu.VMEM((here, 2 * width), BF16),
            pltpu.VMEM((total // LANES, 8, LANES), F32),
            pltpu.VMEM((n, 8, LANES), F32),
            pltpu.VMEM((n, 8, LANES), F32),
            pltpu.VMEM((n, cap, width), F32),
            pltpu.VMEM((n, cap, width), F32),
            pltpu.VMEM((ET_OWN + PT_OWN, total), BF16),
            pltpu.VMEM((np_, ET_OWN, width), F32),
            pltpu.VMEM((ne, PT_OWN, width), F32),
            dma((chunks,)), dma((chunks,)),
            dma((n,)), dma((n,)), dma((n,)), dma((n,)),
            dma((np_,)), dma((np_,)), dma((ne,)), dma((ne,)),
        ],
        compiler_params=pltpu.CompilerParams(
            collective_id=0, has_side_effects=True, vmem_limit_bytes=50 * 1024 * 1024
        ),
    )(
        images, w_first, w_second, calib_scale, calib_bias,
        template_slot.reshape(1, here), media_counts,
    )


def solution(mesh):
    ne, np_ = mesh.shape["enrol"], mesh.shape["probe"]
    return jax.shard_map(
        functools.partial(shards, ne, np_),
        mesh=mesh,
        in_specs=(
            P(("groups", "enrol", "probe"), None),
            P(),
            P(),
            P(),
            P(),
            P(("groups", "enrol", "probe")),
            P(("groups", "enrol", "probe"), None),
        ),
        out_specs=P(("groups", "enrol"), "probe"),
        check_vma=False,
    )
```

time: 93 us -> 61.2 us (0.66)
  Pallas kernels: 0 us -> 54.6 us
  blocking collectives: 23.2 us -> 0 us
  waiting for transfers between devices: 20.4 us -> 0 us
  matrix products: 16 us -> 0 us
  starting transfers between devices: 13.4 us -> 0 us
  local copies, waits for them, and re-layouts: 12.7 us -> 4.85 us
  other arithmetic: 5.57 us -> 0 us
    pallas_call x0 -> x1, Pallas kernels: none -> 54.6 us  [shards(): pl.pallas_call(functools.partial(kernel, ne, np_, chunk), out_shape=jax.S...]
    all_gather x2 -> x0, blocking collectives: 23.2 us -> none  [the longest x1 15.4 us: shards(): lax.all_gather(probe_own, 'enrol', axis=0, tiled=True)]
    all_to_all x2 -> x0, waiting for transfers between devices: 20.4 us -> none  [the longest x1 20.4 us: shards(): lax.all_to_all(send_rows, ('enrol', 'probe'), split_axis=0, concat_axis=0...]
    dot_general x4 -> x0, matrix products: 16 us -> none  [the longest x1 8.8 us: shards(): jnp.dot(images, w_first, precision=HIGH, preferred_element_type=jnp.float32)]
    all_to_all x2 -> x0, starting transfers between devices: 13.4 us -> none  [the longest x1 7.36 us: shards(): lax.all_to_all(send_slots, ('enrol', 'probe'), split_axis=0, concat_axis=...]
    gather x2 -> x0, local copies, waits for them, and re-layouts: 10.8 us -> none  [the longest x1 6.18 us: shards(): template_slot[picked].reshape(owners, capacity)]
    unnamed x6 -> x9, local copies, waits for them, and re-layouts: 0.01 us -> 4.85 us
    mul x3 -> x0, other arithmetic: 2.58 us -> none  [the longest x1 2.42 us: shards(): embedding[picked].reshape(owners, capacity, width)]
  transfers between devices with their start and end apart: 2 -> 0, of which waited for: 1 -> 0; matrix products, arithmetic and copies ran while one was open for 24% -> 0% of each run, Pallas kernels for 0% -> 0%
where the time goes in v1:
time: 61.2 us; the launch traced here: 60.8 us
  Pallas kernels  54.6 us (89%)
  local copies, waits for them, and re-layouts  4.85 us (8%)
  between operations  1.32 us (2%)
    pallas_call x1, Pallas kernels, shards(): pl.pallas_call(functools.partial(kernel, ne, np_, chunk), out_shape=jax.S...  54.6 us
    unnamed x9, local copies, waits for them, and re-layouts  4.85 us

profile of v1, /device:TPU:0, one launch (start us, length us, event | category | flops | bytes accessed | tf_op | source)
XLA Modules:
  0.0 60.8 jit_solution(5935744732082469820)
XLA Ops:
  1.3 0.0 copy-start
  1.3 1.6 %copy-done = f32[2048,256]{1,0:T(8,128)S(1)} copy-done((f32[2048,256]{1,0:T(8,128)S(1)}, f32[2048,256]{1,0:T(8,128)}, u32[]{:S(2)}) %copy-start) | copy-done | bytes 2097176
  2.9 0.0 copy-start.1
  2.9 1.2 %copy-done.1 = f32[512,512]{1,0:T(8,128)S(1)} copy-done((f32[512,512]{1,0:T(8,128)S(1)}, f32[512,512]{1,0:T(8,128)}, u32[]{:S(2)}) %copy-start.1) | copy-done | bytes 1048600
  4.1 0.0 copy-start.2
  4.1 0.7 %copy-done.2 = s32[512]{0:T(512)S(1)} copy-done((s32[512]{0:T(512)S(1)}, s32[512]{0:T(512)}, u32[]{:S(2)}) %copy-start.2) | copy-done | bytes 2072
  4.8 0.0 copy-start.3
  4.8 0.7 %copy-done.3 = s32[1,16]{1,0:T(1,128)S(1)} copy-done((s32[1,16]{1,0:T(1,128)S(1)}, s32[1,16]{1,0:T(1,128)}, u32[]{:S(2)}) %copy-start.3) | copy-done | bytes 88
  5.5 54.6 %shard_map.73 = bf16[512,256]{1,0:T(8,128)(2,1)S(1)} custom-call(f32[512,512]{1,0:T(8,128)S(1)} %copy-done.1, f32[512,2048]{1,0:T(8,128)} %w_first.1, f32[2048,256]{1,0:T(8,128)S(1)} %copy-done, f32[1]{0:T(128)S(6)} %copy.9.scale, f32[1]{0:T(128)S(6)} %copy.10.bias, s32[1,512]{1,0:T(1,128)S(1)} %bitcast.1, s32[1,16]{1,0:T(1,128)S(1)} %copy-done.3), custom_call_target="tpu_custom_call" | custom-call | tf_op jit(solution)/shard_map/pallas_call | solution.py:256
  60.1 0.7 %copy.11 = bf16[512,256]{1,0:T(8,128)(2,1)} copy(bf16[512,256]{1,0:T(8,128)(2,1)S(1)} %shard_map.73) | data formatting | bytes 524288
Async XLA Ops:
  1.3 1.6 %copy-start = (f32[2048,256]{1,0:T(8,128)S(1)}, f32[2048,256]{1,0:T(8,128)}, u32[]{:S(2)}) copy-start(f32[2048,256]{1,0:T(8,128)} %w_second.1) | copy-start | bytes 6291460
  2.9 1.2 %copy-start.1 = (f32[512,512]{1,0:T(8,128)S(1)}, f32[512,512]{1,0:T(8,128)}, u32[]{:S(2)}) copy-start(f32[512,512]{1,0:T(8,128)} %images.1) | copy-start | bytes 3145732
  4.1 0.7 %copy-start.2 = (s32[512]{0:T(512)S(1)}, s32[512]{0:T(512)}, u32[]{:S(2)}) copy-start(s32[512]{0:T(512)} %param.12) | copy-start | bytes 6148
  4.8 0.7 %copy-start.3 = (s32[1,16]{1,0:T(1,128)S(1)}, s32[1,16]{1,0:T(1,128)}, u32[]{:S(2)}) copy-start(s32[1,16]{1,0:T(1,128)} %counts.1) | copy-start | bytes 196

commit v2 on v1

--- a/solution.py
+++ b/solution.py
@@ -32,8 +32,8 @@
     ne, np_, chunk,
     images, w_first, w_second, scale, bias, slots, counts,
     out,
-    w1, w2, gather, catted, slot_tiles, slot_send, slot_recv, send, recv, pool, enrol, probe,
-    w1_sem, w2_sem, ss_sem, sr_sem, rs_sem, rr_sem, es_sem, er_sem, ps_sem, pr_sem,
+    held, w1, w2, w1h, w1l, w2h, w2l, gather, catted, slot_tiles, slot_send, slot_recv, send, recv, pool, enrol, probe,
+    x_sem, w1_sem, w2_sem, ss_sem, sr_sem, rs_sem, rr_sem, es_sem, er_sem, ps_sem, pr_sem,
 ):
     n = ne * np_
     images_here = images.shape[0]
@@ -58,6 +58,15 @@
 
     chunks = w1.shape[0]
     loads = []
+    half_rows = images_here // 2
+    half = ne // 2
+    here = e // half
+    pictures = []
+    for t in range(2):
+        spot = pl.ds(pl.multiple_of((here if t else 1 - here) * half_rows, half_rows), half_rows)
+        a = pltpu.make_async_copy(images.at[spot, :], held.at[t], x_sem.at[t])
+        a.start()
+        pictures.append((spot, a))
     for c in range(chunks):
         a = pltpu.make_async_copy(w_first.at[:, pl.ds(c * chunk, chunk)], w1.at[c], w1_sem.at[c])
         b = pltpu.make_async_copy(w_second.at[pl.ds(c * chunk, chunk), :], w2.at[c], w2_sem.at[c])
@@ -114,42 +123,19 @@
     lax.fori_loop(1, n, send_slots, 0)
     slot_recv[me] = slot_row(me)
 
-    xh, xl = split(images[...])
-    x3 = jnp.concatenate([xh, xl, xh], axis=1)
-    feature = None
-    for c in range(chunks):
-        loads[c][0].wait()
-        ah, al = split(w1[c])
-        hidden = jax.nn.gelu(
-            jnp.dot(x3, jnp.concatenate([ah, ah, al], axis=0), preferred_element_type=F32)
-        )
-        hh, hl = split(hidden)
-        loads[c][1].wait()
-        bh, bl = split(w2[c])
-        part = jnp.dot(
-            jnp.concatenate([hh, hl, hh], axis=1),
-            jnp.concatenate([bh, bh, bl], axis=0),
-            preferred_element_type=F32,
-        )
-        feature = part if feature is None else feature + part
-    embedding = feature * lax.rsqrt(jnp.sum(feature * feature, axis=-1, keepdims=True) + 1e-06)
-    h, l = split(embedding)
-    catted[:, :width] = h
-    catted[:, width:] = l
-
-    half = ne // 2
-    here = e // half
     per_row = np_ * cap
-    for t in range(ne):
+    early = ne // 4
+
+    def send_row(t, spot):
         if t < half:
-            er = (1 - here) * half + lax.rem(e + t, half)
+            er = (1 - here) * (ne - 1 - t) + here * t
         else:
             er = here * half + lax.rem(e + 1 + t - half, half)
-        picked = jnp.dot(
-            gather[pl.ds(pl.multiple_of(er * per_row, per_row), per_row), :],
-            catted[...],
-            preferred_element_type=F32,
-        )
+        span = pl.ds(pl.multiple_of(er * per_row, per_row), per_row)
+        if spot is None:
+            picked = jnp.dot(gather[span, :], catted[...], preferred_element_type=F32)
+        else:
+            picked = jnp.dot(gather[span, spot], catted[spot, :], preferred_element_type=F32)
         picked = (picked[:, :width] + picked[:, width:]).reshape(np_, cap, width)
         send[pl.ds(er * np_, np_)] = picked
         if t < ne - 1:
@@ -159,6 +145,41 @@
             for k in range(1, np_):
                 row_copy(er * np_ + lax.rem(p + k, np_), me).start()
             recv[me] = send[me]
+
+    for t in range(2):
+        spot, arrival = pictures[t]
+        arrival.wait()
+        xh, xl = split(held[t])
+        x3 = jnp.concatenate([xh, xl, xh], axis=1)
+        feature = None
+        for c in range(chunks):
+            if t == 0:
+                loads[c][0].wait()
+                ah, al = split(w1[c])
+                w1h[c], w1l[c] = ah, al
+            else:
+                ah, al = w1h[c], w1l[c]
+            hidden = jax.nn.gelu(
+                jnp.dot(x3, jnp.concatenate([ah, ah, al], axis=0), preferred_element_type=F32)
+            )
+            hh, hl = split(hidden)
+            if t == 0:
+                loads[c][1].wait()
+                bh, bl = split(w2[c])
+                w2h[c], w2l[c] = bh, bl
+            else:
+                bh, bl = w2h[c], w2l[c]
+            part = jnp.dot(
+                jnp.concatenate([hh, hl, hh], axis=1),
+                jnp.concatenate([bh, bh, bl], axis=0),
+                preferred_element_type=F32,
+            )
+            feature = part if feature is None else feature + part
+        embedding = feature * lax.rsqrt(jnp.sum(feature * feature, axis=-1, keepdims=True) + 1e-06)
+        h, l = split(embedding)
+        catted[spot, :] = jnp.concatenate([h, l], axis=1)
+        for u in range(early) if t == 0 else range(early, ne):
+            send_row(u, spot if t == 0 else None)
 
     def slots_in(k, c):
         o = lax.rem(me + k, n)
@@ -251,16 +272,21 @@
     chunks = hidden // chunk
     vmem = pl.BlockSpec(memory_space=pltpu.VMEM)
     smem = pl.BlockSpec(memory_space=pltpu.SMEM)
-    anywhere = pl.BlockSpec(memory_space=pl.ANY)
+    hbm = pl.BlockSpec(memory_space=pltpu.HBM)
     dma = pltpu.SemaphoreType.DMA
     return pl.pallas_call(
         functools.partial(kernel, ne, np_, chunk),
         out_shape=jax.ShapeDtypeStruct((np_ * ET_OWN, ne * PT_OWN), BF16),
-        in_specs=[vmem, anywhere, anywhere, smem, smem, vmem, smem],
+        in_specs=[hbm, hbm, hbm, smem, smem, vmem, smem],
         out_specs=vmem,
         scratch_shapes=[
+            pltpu.VMEM((2, here // 2, features), F32),
             pltpu.VMEM((chunks, features, chunk), F32),
             pltpu.VMEM((chunks, chunk, width), F32),
+            pltpu.VMEM((chunks, features, chunk), BF16),
+            pltpu.VMEM((chunks, features, chunk), BF16),
+            pltpu.VMEM((chunks, chunk, width), BF16),
+            pltpu.VMEM((chunks, chunk, width), BF16),
             pltpu.VMEM((total, here), BF16),
             pltpu.VMEM((here, 2 * width), BF16),
             pltpu.VMEM((total // LANES, 8, LANES), F32),
@@ -271,12 +297,12 @@
             pltpu.VMEM((ET_OWN + PT_OWN, total), BF16),
             pltpu.VMEM((np_, ET_OWN, width), F32),
             pltpu.VMEM((ne, PT_OWN, width), F32),
-            dma((chunks,)), dma((chunks,)),
+            dma((2,)), dma((chunks,)), dma((chunks,)),
             dma((n,)), dma((n,)), dma((n,)), dma((n,)),
             dma((np_,)), dma((np_,)), dma((ne,)), dma((ne,)),
         ],
         compiler_params=pltpu.CompilerParams(
-            collective_id=0, has_side_effects=True, vmem_limit_bytes=50 * 1024 * 1024
+            collective_id=0, has_side_effects=True, vmem_limit_bytes=60 * 1024 * 1024
         ),
     )(
         images, w_first, w_second, calib_scale, calib_bias,

time: 61.2 us -> 53.6 us (0.88)
  Pallas kernels: 54.6 us -> 50.3 us
  local copies, waits for them, and re-layouts: 4.85 us -> 1.67 us
    pallas_call x1, Pallas kernels: 54.6 us -> 50.3 us  [shards(): pl.pallas_call(functools.partial(kernel, ne, np_, chunk), out_shape=jax.S...]
    unnamed x9 -> x1, local copies, waits for them, and re-layouts: 4.85 us -> 1.67 us
where the time goes in v2:
time: 53.6 us; the launch traced here: 53.3 us
  Pallas kernels  50.3 us (94%)
  local copies, waits for them, and re-layouts  1.67 us (3%)
  between operations  1.3 us (2%)
    pallas_call x1, Pallas kernels, shards(): pl.pallas_call(functools.partial(kernel, ne, np_, chunk), out_shape=jax.S...  50.3 us
    unnamed x1, local copies, waits for them, and re-layouts  1.67 us

profile of v2, /device:TPU:0, one launch (start us, length us, event | category | flops | bytes accessed | tf_op | source)
XLA Modules:
  0.0 53.3 jit_solution(9079847879772439071)
XLA Ops:
  1.3 50.3 %shard_map.73 = bf16[512,256]{1,0:T(8,128)(2,1)} custom-call(f32[512,512]{1,0:T(8,128)} %images.1, f32[512,2048]{1,0:T(8,128)} %w_first.1, f32[2048,256]{1,0:T(8,128)} %w_second.1, f32[1]{0:T(128)S(6)} %copy.9.scale, f32[1]{0:T(128)S(6)} %copy.10.bias, s32[1,512]{1,0:T(1,128)} %bitcast.1, s32[1,16]{1,0:T(1,128)} %counts.1), custom_call_target="tpu_custom_call" | custom-call | tf_op jit(solution)/shard_map/pallas_call | solution.py:277
  51.6 1.7 %copy.11 = bf16[512,256]{1,0:T(8,128)(2,1)} copy(bf16[512,256]{1,0:T(8,128)(2,1)} %shard_map.73) | data formatting | bytes 524288
